TPU v7x, 256 devices: a whole 4x4x8 slice. The times are simulated.
256 devices in a mesh: lat: 16 (over z, x_hi), lon: 16 (over y, x_lo, core).
Axes of the slice: x: 4 (x_hi: 2, x_lo: 2; x = x_hi * 2 + x_lo), y: 4, z: 8, core: 2. Of those that a mesh axis runs over, the one named last changes fastest.
Arguments:
- features: bfloat16 [192, 720, 256], P('lat', 'lon'), may hold values from -6 to 6
- cotangent: bfloat16 [192, 720, 256], P('lat', 'lon'), may hold values from -6 to 6
- weights: bfloat16 [9, 256, 256], replicated, may hold values from -0.125 to 0.125
- quad_weights: bfloat16 [9, 192, 9, 17], replicated, may hold values from -0.71875 to 0.71875
- reach_table: int32 [192, 9], replicated, may hold values from 1 to 8
Outputs:
- grad_input: bfloat16 [192, 720, 256], P('lat', 'lon')
- grad_weight: float32 [9, 256, 256], replicated
All inputs are finite; a program needn't handle non-finite values.
Results may differ from a plain program's by a relative error of at most 0.0065.
Values may be sent and summed in bfloat16 or wider, within the bound.
No kernel may reach another device: no remote copies, remote signals or barrier semaphores. Data moves between devices by JAX's collectives and lax.ppermute only.
A program may use at most 192 MiB of HBM per device.

v0:
```python
import functools
import math

import jax
import jax.numpy as jnp
from jax import lax
from jax.experimental import pallas as pl
from jax.experimental.pallas import tpu as pltpu
from jax.sharding import PartitionSpec as P

F32 = jnp.float32
BF16 = jnp.bfloat16
BOTH = ("lat", "lon")
WIDE = 48
WIN = 32


def coords(index):
    lat, lon = divmod(index, 16)
    return {"z": lat // 2, "x": lat % 2 * 2 + lon // 2 % 2, "y": lon // 4, "c": lon % 2}


def index_of(at):
    return (at["z"] * 2 + at["x"] // 2) * 16 + at["y"] * 4 + at["x"] % 2 * 2 + at["c"]


def route(**moves):
    pairs = []
    for source in range(256):
        at = coords(source)
        for axis, move in moves.items():
            at[axis] = move(at[axis])
        pairs.append((source, index_of(at)))
    return pairs


def flip(v):
    return v ^ 1


CORE = route(c=flip)
SLABS = [
    [i for i in range(256) if coords(i)["z"] // 2 == pair and coords(i)["c"] == c]
    for pair in range(4)
    for c in range(2)
]
QUAD = [route(z=lambda v, m=m: v ^ m) for m in (2, 4, 6)]


def chain(odd, periodic):
    pairs = [(i, ((i + odd) ^ 1) - odd) for i in range(16)]
    return [(i, j % 16) for i, j in pairs if periodic or 0 <= j < 16]


def send(value, pairs):
    return lax.ppermute(value, BOTH, pairs)


def trade(blocks):
    return lax.all_to_all(blocks, BOTH, 0, 0, axis_index_groups=SLABS, tiled=True)


def whole(n):
    return [pl.BlockSpec(memory_space=pltpu.VMEM)] * n


ANY = pl.BlockSpec(memory_space=pl.ANY)
PARAMS = pltpu.CompilerParams(vmem_limit_bytes=16 * 1024 * 1024)


def groups(u):
    return max(0, 2 * u - 4) // 4, min(11, 2 * u + 5) // 4


def rim_kernel(block_ref, even_ref, odd_ref, ext_ref):
    first = core_of() == 0
    west, east = block_ref[:, :8], block_ref[:, 37:]
    even_ref[...] = jnp.where(first, east, west)
    odd_ref[...] = jnp.where(first, west, east)
    ext_ref[...] = jnp.zeros_like(ext_ref)
    ext_ref[:, 8:53] = block_ref[...]


def extend_kernel(block_ref, even_ref, odd_ref, ext_ref, to_even_ref, to_odd_ref):
    first = core_of() == 0
    even, odd = even_ref[...], odd_ref[...]
    ext_ref[...] = block_ref[...]
    ext_ref[:, :8] = jnp.where(first, odd, even)
    ext_ref[:, 53:61] = jnp.where(first, even, odd)
    top, bottom = ext_ref[:4], ext_ref[8:]
    upper = lax.axis_index("lat") % 2 == 0
    to_even_ref[...] = jnp.where(upper, bottom, top)
    to_odd_ref[...] = jnp.where(upper, top, bottom)


def band_kernel(quad_ref, reach_ref, feat_ref, band_ref, rim_ref, middle_ref, edge_ref, wide_ref, flat_ref, turn_ref):
    wide_ref[...] = jnp.zeros_like(wide_ref)
    wide_ref[:, :45, :] = feat_ref[...]
    middle_ref[...] = wide_ref[4:8].reshape(4 * WIDE, 256).T
    edge = jnp.concatenate([wide_ref[:4], wide_ref[8:]], axis=0)
    edge_ref[...] = edge.reshape(8 * WIDE, 256).T
    flat_ref[...] = jnp.zeros_like(flat_ref)
    taps = lax.broadcasted_iota(jnp.int32, (17, 192), 0)
    for a in range(9):
        keep = jnp.abs(taps - 8) <= reach_ref[a : a + 1, :]
        for k in range(9):
            first = (9 * k + a) * WIN
            line = jnp.where(keep, quad_ref[k, a].astype(F32), 0.0)
            flat_ref[first : first + 17, :] = line.astype(BF16)
    row = lax.axis_index("lat") * 12 - 4 + lax.broadcasted_iota(jnp.int32, (32, 192), 0)
    pick = (row == lax.broadcasted_iota(jnp.int32, (32, 192), 1)).astype(F32).astype(BF16)
    picked = lax.dot_general(
        pick, flat_ref[...], (((1,), (1,)), ((), ())), preferred_element_type=F32
    ).astype(BF16)
    r = lax.broadcasted_iota(jnp.int32, (128, 512), 0)
    c = lax.broadcasted_iota(jnp.int32, (128, 512), 1)
    turn = (r // WIN == c // 128) & (r % WIN + c % WIN == 16)
    turn = turn.astype(F32).astype(BF16)
    for m in range(21):
        part = jnp.dot(picked[:, 128 * m : 128 * m + 128], turn, preferred_element_type=F32)
        for i in range(4):
            turn_ref[4 * m + i] = part[:, 128 * i : 128 * i + 128]
    place = lax.broadcasted_iota(jnp.int32, (16, 128), 1) // WIN

    def spread(p, k, start):
        total = jnp.zeros((16, 128), F32)
        for s in range(4):
            tap = p - start - s + 8
            if 0 <= tap <= 8:
                line = turn_ref[9 * k + tap, start + s : start + s + 1, :]
                total = jnp.where(place == s, jnp.broadcast_to(line, (16, 128)), total)
        return pltpu.roll(total, 0, 1, stride=1, stride_axis=0).astype(BF16)

    for u in range(6):
        low, high = groups(u)
        for pp in range(2):
            p = 2 * u + pp
            for k in range(9):
                first = (pp * 9 + k) * 16
                for g in range(low, high + 1):
                    lanes = slice(128 * g, 128 * g + 128)
                    band_ref[u, first : first + 16, lanes] = spread(p, k, 4 + 4 * g)
                if u in (0, 1, 4, 5):
                    rim_ref[u if u < 2 else u - 2, first : first + 16, :] = spread(p, k, 0 if u < 2 else 16)


def core_of():
    return lax.axis_index("lon") % 2


def halves_of(ref):
    core = core_of()
    own = pl.multiple_of(core * 128, 128)
    other = pl.multiple_of(128 - core * 128, 128)
    return jnp.concatenate([ref[pl.ds(own, 128), :], ref[pl.ds(other, 128), :]], axis=0)


def own_kernel(ext_ref, band_ref, feat_ref, y_ref, sums_ref, part_ref):
    for u in range(6):
        low, high = groups(u)
        band = band_ref[u, :, 128 * low : 128 * high + 128]
        for t in range(3):
            window = ext_ref[4 * low : 4 * high + 4, 16 * t : 16 * t + WIN, :].reshape(-1, 256)
            rows = jnp.dot(band, window, preferred_element_type=F32)
            if u in (2, 3):
                rows = rows.astype(BF16)
            for pp in range(2):
                start = (2 * u + pp) % 4 * WIDE + 16 * t
                for k in range(9):
                    first = (pp * 9 + k) * 16
                    if u in (2, 3):
                        y_ref[k, start : start + 16, :] = rows[first : first + 16]
            if u not in (2, 3):
                sums_ref[u if u < 2 else u - 2, t] = rows
    feat = halves_of(feat_ref)
    for k in range(9):
        part_ref[k] = jnp.dot(feat, y_ref[k], preferred_element_type=F32)


def edge_kernel(even_ref, odd_ref, rim_ref, sums_ref, part_ref, feat_ref, y_ref, send_ref):
    upper = lax.axis_index("lat") % 2 == 0
    for half in range(2):
        block = jnp.where(upper, odd_ref[...], even_ref[...])
        if half:
            block = jnp.where(upper, even_ref[...], odd_ref[...])
        for v in (2 * half, 2 * half + 1):
            rim = rim_ref[v]
            for t in range(3):
                window = block[:, 16 * t : 16 * t + WIN, :].reshape(-1, 256)
                rows = sums_ref[v, t] + jnp.dot(rim, window, preferred_element_type=F32)
                rows = rows.astype(BF16)
                for pp in range(2):
                    start = (2 * v + pp) * WIDE + 16 * t
                    for k in range(9):
                        first = (pp * 9 + k) * 16
                        y_ref[k, start : start + 16, :] = rows[first : first + 16]
    other = feat_ref[pl.ds(pl.multiple_of(128 - core_of() * 128, 128), 128), :]
    for k in range(9):
        part = part_ref[k, 128:] + jnp.dot(other, y_ref[k], preferred_element_type=F32)
        send_ref[k] = part.astype(BF16)


def keep_kernel(y_ref, part_ref, feat_ref, keep_ref):
    own = feat_ref[pl.ds(pl.multiple_of(core_of() * 128, 128), 128), :]
    for k in range(9):
        keep_ref[k] = part_ref[k, :128] + jnp.dot(own, y_ref[k], preferred_element_type=F32)


def input_kernel(middle_ref, edge_ref, w_ref, out_ref):
    def mixed(ref, rows):
        total = jnp.zeros((rows * WIDE, 256), F32)
        for k in range(9):
            total += lax.dot_general(
                ref[k], w_ref[k], (((1,), (1,)), ((), ())), preferred_element_type=F32
            )
        return total.reshape(rows, WIDE, 256)[:, :45].astype(BF16)

    out_ref[4:8] = mixed(middle_ref, 4)
    edge = mixed(edge_ref, 8)
    out_ref[:4] = edge[:4]
    out_ref[8:] = edge[4:]


def split_kernel(keep_ref, got_ref, out_ref):
    for i in range(16):
        rows, cols = slice(i // 2 * 16, i // 2 * 16 + 16), slice(i % 2 * 128, i % 2 * 128 + 128)
        part = keep_ref[:, rows, cols] + got_ref[:, rows, cols].astype(F32)
        j = i // 2 * 4 + i % 2
        out_ref[j] = part[:, :8].astype(BF16)
        out_ref[j + 2] = part[:, 8:].astype(BF16)


def sum_kernel(got_ref, out_ref):
    total = got_ref[0].astype(F32)
    for j in range(1, 32):
        total = total + got_ref[j].astype(F32)
    out_ref[...] = total.astype(BF16)


def join_kernel(scale, other, blocks_ref, *refs):
    out_ref, half_ref, sem = refs[-3:]
    start = pl.multiple_of((core_of() ^ other) * 128, 128)
    for j in range(32):
        rows, cols = slice(j // 2 * 8, j // 2 * 8 + 8), slice(j % 2 * 128, j % 2 * 128 + 128)
        half_ref[:, rows, cols] = blocks_ref[j].astype(F32) * scale
    copy = pltpu.make_async_copy(half_ref, out_ref.at[:, pl.ds(start, 128), :], sem)
    copy.start()
    copy.wait()


def call(kernel, outs, specs, *args, out_spec=None, scratch=(), aliases=None, **cost):
    estimate = pl.CostEstimate(transcendentals=0, **cost) if cost else None
    out_spec = out_spec or pl.BlockSpec(memory_space=pltpu.VMEM)
    return pl.pallas_call(
        kernel,
        out_shape=outs,
        in_specs=specs,
        out_specs=jax.tree.map(lambda _: out_spec, outs),
        scratch_shapes=scratch,
        input_output_aliases=aliases or {},
        compiler_params=PARAMS,
        cost_estimate=estimate,
    )(*args)


def shape(dims, dtype):
    return jax.ShapeDtypeStruct(dims, dtype)


def local(features, cotangent, weights, quad_weights, reach_table):
    slab = shape((12, 8, 256), BF16)
    even, odd, ext = call(
        rim_kernel, (slab, slab, shape((12, 64, 256), BF16)), whole(1), cotangent,
        flops=2 * 10**10, bytes_accessed=10**6,
    )
    even = lax.ppermute(even, "lon", chain(0, True))
    odd = lax.ppermute(odd, "lon", chain(1, True))
    band, rims, feat, feat_edge = call(
        band_kernel,
        (
            shape((6, 288, 12 * WIN), BF16), shape((4, 288, 4 * WIN), BF16),
            shape((256, 4 * WIDE), BF16), shape((256, 8 * WIDE), BF16),
        ),
        whole(3), quad_weights.transpose(0, 2, 3, 1), reach_table.T, features,
        scratch=[
            pltpu.VMEM((12, WIDE, 256), BF16), pltpu.VMEM((84 * WIN, 192), BF16), pltpu.VMEM((84, 32, 128), F32),
        ],
    )
    even, odd, band = lax.optimization_barrier((even, odd, band))
    rim = shape((4, 64, 256), BF16)
    ext, even, odd = call(
        extend_kernel, (shape((12, 64, 256), BF16), rim, rim), whole(3), ext, even, odd
    )
    even = lax.ppermute(even, "lat", chain(0, False))
    odd = lax.ppermute(odd, "lat", chain(1, False))
    y, sums, part = call(
        own_kernel,
        (shape((9, 4 * WIDE, 256), BF16), shape((4, 3, 288, 256), F32), shape((9, 256, 256), F32)),
        whole(3), ext, band, feat, flops=10**6, bytes_accessed=10**6,
    )
    even, odd, part = lax.optimization_barrier((even, odd, part))
    halves, blocks = (9, 128, 256), (32, 9, 8, 128)
    y_edge, out = call(
        edge_kernel, (shape((9, 8 * WIDE, 256), BF16), shape(halves, BF16)), whole(6),
        even, odd, rims, sums, part, feat_edge,
    )
    got = send(out, CORE)
    keep = call(
        keep_kernel, shape(halves, F32), whole(3), y_edge, part, feat_edge,
        flops=10**9, bytes_accessed=4 * 10**6,
    )
    got = trade(call(split_kernel, shape(blocks, BF16), whole(2), keep, got))
    mine = call(sum_kernel, shape(blocks[1:], BF16), whole(1), got)
    mine, y, y_edge = lax.optimization_barrier((mine, y, y_edge))
    gots = [send(mine, r).astype(F32) for r in QUAD]
    total = (mine.astype(F32) + gots[0]) + (gots[1] + gots[2])
    grad_input = call(
        input_kernel, shape((12, 45, 256), BF16), whole(3), y, y_edge, weights,
        flops=2 * 10**9, bytes_accessed=4 * 10**6,
    )
    total, grad_input = lax.optimization_barrier((total, grad_input))
    own = trade(jnp.broadcast_to(total.astype(BF16), blocks))
    got = send(own, CORE)
    scale = 1.0 / math.sqrt(192 * 720)
    scratch = [pltpu.VMEM(halves, F32), pltpu.SemaphoreType.DMA]
    full = shape((9, 256, 256), F32)
    grad_weight = call(
        functools.partial(join_kernel, scale, 0), full, whole(1), own,
        out_spec=ANY, scratch=scratch, flops=10**6, bytes_accessed=2 * 10**6,
    )
    grad_weight = call(
        functools.partial(join_kernel, scale, 1), full, whole(1) + [ANY], got, grad_weight,
        out_spec=ANY, scratch=scratch, aliases={1: 0}, flops=10**6, bytes_accessed=2 * 10**6,
    )
    return grad_input, grad_weight


def solution(mesh):
    return jax.shard_map(
        local,
        mesh=mesh,
        in_specs=(P("lat", "lon", None), P("lat", "lon", None), P(), P(), P()),
        out_specs=(P("lat", "lon", None), P()),
        check_vma=False,
    )
```

profile of v0, /device:TPU:1, one launch (start us, length us, event | category | flops | bytes accessed | tf_op | source)
XLA Modules:
  0.0 74.3 jit_solution(9255601123281570634)
XLA Ops:
  0.6 0.0 copy-start.2
  0.6 0.0 copy-start
  0.7 0.0 copy-start.1
  0.7 0.0 copy-start.4
  0.7 1.1 %copy-done.4 = bf16[12,45,256]{2,1,0:T(8,128)(2,1)S(1)} copy-done((bf16[12,45,256]{2,1,0:T(8,128)(2,1)S(1)}, bf16[12,45,256]{2,1,0:T(8,128)(2,1)}, u32[]{:S(2)}) %copy-start.4) | copy-done | bytes 276504
  1.7 0.1 shard_map.68
  1.8 3.3 %collective-permute-start = (bf16[12,8,256]{2,1,0:T(8,128)(2,1)S(1)}, bf16[12,8,256]{2,1,0:T(8,128)(2,1)S(1)}, u32[]{:S(2)}, u32[]{:S(2)}) collective-permute-start(bf16[12,8,256]{2,1,0:T(8,128)(2,1)S(1)} %get-tuple-element.29), channel_id=1, source_target_pairs={{0,1},{1,0},{2,3},{3,2},{4,5},{5,4},{6,7},{7,6},{8,9},{9,8},{10,11... | collective-permute-start | bytes 147464 | tf_op jit(solution)/shard_map/ppermute | solution.py:276
  5.1 0.0 collective-permute-start.1
  5.1 0.0 copy-done.2
  5.1 0.0 copy-done
  5.1 0.0 copy-done.1
  5.1 1.2 %shard_map.69 = (bf16[6,288,384]{2,1,0:T(8,128)(2,1)S(1)}, bf16[4,288,128]{2,1,0:T(8,128)(2,1)S(1)}, bf16[256,192]{1,0:T(8,128)(2,1)S(1)}, bf16[256,384]{1,0:T(8,128)(2,1)S(1)}) custom-call(bf16[9,9,17,192]{3,2,1,0:T(8,128)(2,1)S(1)} %bitcast.2, s32[9,192]{1,0:T(8,128)S(1)} %bitcast.3, bf16[12,45,256]{2,1,0:T(8,128)(2,1)S(1)} %copy-done.1), custom_call_target="tpu_custom_call" | custom-call | tf_op jit(solution)/shard_map/pallas_call | solution.py:254
  6.4 0.0 collective-permute-done.even_ref
  6.4 2.3 %collective-permute-done.1.odd_ref = bf16[12,8,256]{2,1,0:T(8,128)(2,1)S(1)} collective-permute-done((bf16[12,8,256]{2,1,0:T(8,128)(2,1)S(1)}, bf16[12,8,256]{2,1,0:T(8,128)(2,1)S(1)}, u32[]{:S(2)}, u32[]{:S(2)}) %collective-permute-start.1) | collective-permute-done | bytes 49184 | tf_op jit(solution)/shard_map/ppermute | solution.py:277
  8.6 0.1 shard_map.70
  8.7 1.3 %collective-permute-start.2 = (bf16[4,64,256]{2,1,0:T(8,128)(2,1)S(1)}, bf16[4,64,256]{2,1,0:T(8,128)(2,1)S(1)}, u32[]{:S(2)}, u32[]{:S(2)}) collective-permute-start(bf16[4,64,256]{2,1,0:T(8,128)(2,1)S(1)} %get-tuple-element.34), channel_id=1, source_target_pairs={{0,16},{16,0},{32,48},{48,32},{64,80},{80,64},{96,112},{112,96},{1... | collective-permute-start | bytes 393224 | tf_op jit(solution)/shard_map/ppermute | solution.py:294
  10.0 0.7 collective-permute-start.3
  10.7 1.4 %shard_map.71 = (bf16[9,192,256]{2,1,0:T(8,128)(2,1)S(1)}, f32[4,3,288,256]{3,2,1,0:T(8,128)S(1)}, f32[9,256,256]{2,1,0:T(8,128)S(1)}) custom-call(bf16[12,64,256]{2,1,0:T(8,128)(2,1)S(1)} %get-tuple-element.36.ext_ref, bf16[6,288,384]{2,1,0:T(8,128)(2,1)S(1)} %get-tuple-element.37.band_ref, bf16[256,192]{1,0:T(8,128)(2,1)S(1)} %get-tuple-element.38.feat_ref), custom_call_target="tpu_custom_call" | custom-call | flops 1000000 | bytes 1000000 | tf_op jit(solution)/shard_map/pallas_call | solution.py:254
  12.1 2.1 %collective-permute-done.2.even_ref = bf16[4,64,256]{2,1,0:T(8,128)(2,1)S(1)} collective-permute-done((bf16[4,64,256]{2,1,0:T(8,128)(2,1)S(1)}, bf16[4,64,256]{2,1,0:T(8,128)(2,1)S(1)}, u32[]{:S(2)}, u32[]{:S(2)}) %collective-permute-start.2) | collective-permute-done | bytes 131104 | tf_op jit(solution)/shard_map/ppermute | solution.py:294
  14.1 0.0 collective-permute-done.3.odd_ref
  14.1 1.1 %shard_map.72 = (bf16[9,384,256]{2,1,0:T(8,128)(2,1)S(1)}, bf16[9,128,256]{2,1,0:T(8,128)(2,1)S(1)}) custom-call(bf16[4,64,256]{2,1,0:T(8,128)(2,1)S(1)} %collective-permute-done.2.even_ref, bf16[4,64,256]{2,1,0:T(8,128)(2,1)S(1)} %collective-permute-done.3.odd_ref, bf16[4,288,128]{2,1,0:T(8,128)(2,1)S(1)} %get-tuple-element.42.rim_ref, ...), custom_call_target="tpu_custom_call" | custom-call | tf_op jit(solution)/shard_map/pallas_call | solution.py:254
  15.2 3.4 %collective-permute-start.4 = (bf16[9,128,256]{2,1,0:T(8,128)(2,1)S(1)}, bf16[9,128,256]{2,1,0:T(8,128)(2,1)S(1)}, u32[]{:S(2)}, u32[]{:S(2)}) collective-permute-start(bf16[9,128,256]{2,1,0:T(8,128)(2,1)S(1)} %get-tuple-element.47), channel_id=1, source_target_pairs={{0,1},{1,0},{2,3},{3,2},{4,5},{5,4},{6,7},{7,6},{8,9},{9,8},{10,11... | collective-permute-start | bytes 1769480 | tf_op jit(solution)/shard_map/ppermute | solution.py:56
  18.6 0.5 shard_map.73.keep_ref
  19.1 0.0 copy-start.3
  19.1 1.1 %collective-permute-done.4.got_ref = bf16[9,128,256]{2,1,0:T(8,128)(2,1)S(1)} collective-permute-done((bf16[9,128,256]{2,1,0:T(8,128)(2,1)S(1)}, bf16[9,128,256]{2,1,0:T(8,128)(2,1)S(1)}, u32[]{:S(2)}, u32[]{:S(2)}) %collective-permute-start.4) | collective-permute-done | bytes 589856 | tf_op jit(solution)/shard_map/ppermute | solution.py:56
  20.3 0.1 shard_map.74
  20.4 21.6 %all_to_all.10.got_ref = bf16[32,9,8,128]{3,2,1,0:T(8,128)(2,1)S(1)} all-to-all(bf16[32,9,8,128]{3,2,1,0:T(8,128)(2,1)S(1)} %shard_map.74), channel_id=1, replica_groups={{0,2,4,6,8,10,12,14,16,18,20,22,24,26,28,30,32,34,36,38,40,42,44,46,48,..., dimensions={0} | all-to-all | bytes 1179648 | tf_op jit(solution)/shard_map/all_to_all | solution.py:60
  42.0 0.1 shard_map.75
  42.1 4.8 %collective-permute-start.7 = (bf16[9,8,128]{2,1,0:T(8,128)(2,1)S(1)}, bf16[9,8,128]{2,1,0:T(8,128)(2,1)S(1)}, u32[]{:S(2)}, u32[]{:S(2)}) collective-permute-start(bf16[9,8,128]{2,1,0:T(8,128)(2,1)S(1)} %shard_map.75), channel_id=1, source_target_pairs={{0,192},{1,193},{2,194},{3,195},{4,196},{5,197},{6,198},{7,199},{8... | collective-permute-start | bytes 55304 | tf_op jit(solution)/shard_map/ppermute | solution.py:56
  46.8 2.8 %collective-permute-start.6 = (bf16[9,8,128]{2,1,0:T(8,128)(2,1)S(1)}, bf16[9,8,128]{2,1,0:T(8,128)(2,1)S(1)}, u32[]{:S(2)}, u32[]{:S(2)}) collective-permute-start(bf16[9,8,128]{2,1,0:T(8,128)(2,1)S(1)} %shard_map.75), channel_id=1, source_target_pairs={{0,128},{1,129},{2,130},{3,131},{4,132},{5,133},{6,134},{7,135},{8... | collective-permute-start | bytes 55304 | tf_op jit(solution)/shard_map/ppermute | solution.py:56
  49.6 0.0 collective-permute-start.5
  49.6 0.0 copy-done.3
  49.6 1.7 %shard_map.76 = bf16[12,45,256]{2,1,0:T(8,128)(2,1)} custom-call(bf16[9,192,256]{2,1,0:T(8,128)(2,1)S(1)} %get-tuple-element.50.middle_ref, bf16[9,384,256]{2,1,0:T(8,128)(2,1)S(1)} %get-tuple-element.51.y_ref.edge_ref, bf16[9,256,256]{2,1,0:T(8,128)(2,1)S(1)} %copy-done.3), custom_call_target="tpu_custom_call" | custom-call | flops 2000000000 | bytes 4000000 | tf_op jit(solution)/shard_map/pallas_call | solution.py:254
  51.3 0.0 collective-permute-done.7
  51.3 2.0 %collective-permute-done.6 = bf16[9,8,128]{2,1,0:T(8,128)(2,1)S(1)} collective-permute-done((bf16[9,8,128]{2,1,0:T(8,128)(2,1)S(1)}, bf16[9,8,128]{2,1,0:T(8,128)(2,1)S(1)}, u32[]{:S(2)}, u32[]{:S(2)}) %collective-permute-start.6) | collective-permute-done | bytes 18464 | tf_op jit(solution)/shard_map/ppermute | solution.py:56
  53.3 0.0 collective-permute-done.5
  53.4 0.1 broadcast_in_dim.3
  53.4 13.8 %all_to_all.11.blocks_ref = bf16[32,9,8,128]{3,2,1,0:T(8,128)(2,1)S(1)} all-to-all(bf16[32,9,8,128]{3,2,1,0:T(8,128)(2,1)S(1)} %broadcast_in_dim.3), channel_id=1, replica_groups={{0,2,4,6,8,10,12,14,16,18,20,22,24,26,28,30,32,34,36,38,40,42,44,46,48,..., dimensions={0} | all-to-all | bytes 1179648 | tf_op jit(solution)/shard_map/all_to_all | solution.py:60
  67.2 4.4 %collective-permute-start.8 = (bf16[32,9,8,128]{3,2,1,0:T(8,128)(2,1)S(1)}, bf16[32,9,8,128]{3,2,1,0:T(8,128)(2,1)S(1)}, u32[]{:S(2)}, u32[]{:S(2)}) collective-permute-start(bf16[32,9,8,128]{3,2,1,0:T(8,128)(2,1)S(1)} %all_to_all.11.blocks_ref), channel_id=1, source_target_pairs={{0,1},{1,0},{2,3},{3,2},{4,5},{5,4},{6,7},{7,6},{8,9},{9,8},{10,11... | collective-permute-start | bytes 1769480 | tf_op jit(solution)/shard_map/ppermute | solution.py:56
  71.6 1.1 %shard_map.77.refs_0_ = f32[9,256,256]{2,1,0:T(8,128)} custom-call(bf16[32,9,8,128]{3,2,1,0:T(8,128)(2,1)S(1)} %all_to_all.11.blocks_ref), custom_call_target="tpu_custom_call" | custom-call | flops 1000000 | bytes 2000000 | tf_op jit(solution)/shard_map/pallas_call | solution.py:254
  72.7 0.5 collective-permute-done.8.blocks_ref
  73.2 1.1 %shard_map.78 = f32[9,256,256]{2,1,0:T(8,128)} custom-call(bf16[32,9,8,128]{3,2,1,0:T(8,128)(2,1)S(1)} %collective-permute-done.8.blocks_ref, f32[9,256,256]{2,1,0:T(8,128)} %shard_map.77.refs_0_), custom_call_target="tpu_custom_call", output_to_operand_aliasing={{}: (1, {})} | custom-call | flops 1000000 | bytes 2000000 | tf_op jit(solution)/shard_map/pallas_call | solution.py:254
  (1 shorter events, 0.0 us)
Async XLA Ops:
  0.6 4.5 %copy-start.2 = (s32[192,9]{0,1:T(8,128)S(1)}, s32[192,9]{0,1:T(8,128)}, u32[]{:S(2)}) copy-start(s32[192,9]{0,1:T(8,128)} %param.9) | copy-start | bytes 20740
  0.6 4.5 %copy-start = (bf16[9,192,9,17]{1,3,2,0:T(8,128)(2,1)S(1)}, bf16[9,192,9,17]{1,3,2,0:T(8,128)(2,1)}, u32[]{:S(2)}) copy-start(bf16[9,192,9,17]{1,3,2,0:T(8,128)(2,1)} %param.8) | copy-start | bytes 1586308
  0.7 4.5 %copy-start.1 = (bf16[12,45,256]{2,1,0:T(8,128)(2,1)S(1)}, bf16[12,45,256]{2,1,0:T(8,128)(2,1)}, u32[]{:S(2)}) copy-start(bf16[12,45,256]{2,1,0:T(8,128)(2,1)} %feat_ref.1) | copy-start | bytes 829444
  0.7 1.1 %copy-start.4 = (bf16[12,45,256]{2,1,0:T(8,128)(2,1)S(1)}, bf16[12,45,256]{2,1,0:T(8,128)(2,1)}, u32[]{:S(2)}) copy-start(bf16[12,45,256]{2,1,0:T(8,128)(2,1)} %block_ref.1) | copy-start | bytes 829444
  1.8 4.6 %collective-permute-start = (bf16[12,8,256]{2,1,0:T(8,128)(2,1)S(1)}, bf16[12,8,256]{2,1,0:T(8,128)(2,1)S(1)}, u32[]{:S(2)}, u32[]{:S(2)}) collective-permute-start(bf16[12,8,256]{2,1,0:T(8,128)(2,1)S(1)} %get-tuple-element.29), channel_id=1, source_target_pairs={{0,1},{1,0},{2,3},{3,2},{4,5},{5,4},{6,7},{7,6},{8,9},{9,8},{10,11... | collective-permute-start | bytes 147464 | tf_op jit(solution)/shard_map/ppermute | solution.py:276
  5.1 3.5 %collective-permute-start.1 = (bf16[12,8,256]{2,1,0:T(8,128)(2,1)S(1)}, bf16[12,8,256]{2,1,0:T(8,128)(2,1)S(1)}, u32[]{:S(2)}, u32[]{:S(2)}) collective-permute-start(bf16[12,8,256]{2,1,0:T(8,128)(2,1)S(1)} %get-tuple-element.30), channel_id=1, source_target_pairs={{0,15},{1,2},{2,1},{3,4},{4,3},{5,6},{6,5},{7,8},{8,7},{9,10},{10,... | collective-permute-start | bytes 147464 | tf_op jit(solution)/shard_map/ppermute | solution.py:277
  8.7 5.4 %collective-permute-start.2 = (bf16[4,64,256]{2,1,0:T(8,128)(2,1)S(1)}, bf16[4,64,256]{2,1,0:T(8,128)(2,1)S(1)}, u32[]{:S(2)}, u32[]{:S(2)}) collective-permute-start(bf16[4,64,256]{2,1,0:T(8,128)(2,1)S(1)} %get-tuple-element.34), channel_id=1, source_target_pairs={{0,16},{16,0},{32,48},{48,32},{64,80},{80,64},{96,112},{112,96},{1... | collective-permute-start | bytes 393224 | tf_op jit(solution)/shard_map/ppermute | solution.py:294
  10.0 4.1 %collective-permute-start.3 = (bf16[4,64,256]{2,1,0:T(8,128)(2,1)S(1)}, bf16[4,64,256]{2,1,0:T(8,128)(2,1)S(1)}, u32[]{:S(2)}, u32[]{:S(2)}) collective-permute-start(bf16[4,64,256]{2,1,0:T(8,128)(2,1)S(1)} %get-tuple-element.35), channel_id=1, source_target_pairs={{16,32},{32,16},{48,64},{64,48},{80,96},{96,80},{112,128},{128,112... | collective-permute-start | bytes 393224 | tf_op jit(solution)/shard_map/ppermute | solution.py:295
  15.2 5.1 %collective-permute-start.4 = (bf16[9,128,256]{2,1,0:T(8,128)(2,1)S(1)}, bf16[9,128,256]{2,1,0:T(8,128)(2,1)S(1)}, u32[]{:S(2)}, u32[]{:S(2)}) collective-permute-start(bf16[9,128,256]{2,1,0:T(8,128)(2,1)S(1)} %get-tuple-element.47), channel_id=1, source_target_pairs={{0,1},{1,0},{2,3},{3,2},{4,5},{5,4},{6,7},{7,6},{8,9},{9,8},{10,11... | collective-permute-start | bytes 1769480 | tf_op jit(solution)/shard_map/ppermute | solution.py:56
  19.1 30.5 %copy-start.3 = (bf16[9,256,256]{2,1,0:T(8,128)(2,1)S(1)}, bf16[9,256,256]{2,1,0:T(8,128)(2,1)}, u32[]{:S(2)}) copy-start(bf16[9,256,256]{2,1,0:T(8,128)(2,1)} %w_ref.1) | copy-start | bytes 3538948
  42.1 9.3 %collective-permute-start.7 = (bf16[9,8,128]{2,1,0:T(8,128)(2,1)S(1)}, bf16[9,8,128]{2,1,0:T(8,128)(2,1)S(1)}, u32[]{:S(2)}, u32[]{:S(2)}) collective-permute-start(bf16[9,8,128]{2,1,0:T(8,128)(2,1)S(1)} %shard_map.75), channel_id=1, source_target_pairs={{0,192},{1,193},{2,194},{3,195},{4,196},{5,197},{6,198},{7,199},{8... | collective-permute-start | bytes 55304 | tf_op jit(solution)/shard_map/ppermute | solution.py:56
  46.8 6.5 %collective-permute-start.6 = (bf16[9,8,128]{2,1,0:T(8,128)(2,1)S(1)}, bf16[9,8,128]{2,1,0:T(8,128)(2,1)S(1)}, u32[]{:S(2)}, u32[]{:S(2)}) collective-permute-start(bf16[9,8,128]{2,1,0:T(8,128)(2,1)S(1)} %shard_map.75), channel_id=1, source_target_pairs={{0,128},{1,129},{2,130},{3,131},{4,132},{5,133},{6,134},{7,135},{8... | collective-permute-start | bytes 55304 | tf_op jit(solution)/shard_map/ppermute | solution.py:56
  49.6 3.7 %collective-permute-start.5 = (bf16[9,8,128]{2,1,0:T(8,128)(2,1)S(1)}, bf16[9,8,128]{2,1,0:T(8,128)(2,1)S(1)}, u32[]{:S(2)}, u32[]{:S(2)}) collective-permute-start(bf16[9,8,128]{2,1,0:T(8,128)(2,1)S(1)} %shard_map.75), channel_id=1, source_target_pairs={{0,64},{1,65},{2,66},{3,67},{4,68},{5,69},{6,70},{7,71},{8,72},{9,... | collective-permute-start | bytes 55304 | tf_op jit(solution)/shard_map/ppermute | solution.py:56
  67.2 6.0 %collective-permute-start.8 = (bf16[32,9,8,128]{3,2,1,0:T(8,128)(2,1)S(1)}, bf16[32,9,8,128]{3,2,1,0:T(8,128)(2,1)S(1)}, u32[]{:S(2)}, u32[]{:S(2)}) collective-permute-start(bf16[32,9,8,128]{3,2,1,0:T(8,128)(2,1)S(1)} %all_to_all.11.blocks_ref), channel_id=1, source_target_pairs={{0,1},{1,0},{2,3},{3,2},{4,5},{5,4},{6,7},{7,6},{8,9},{9,8},{10,11... | collective-permute-start | bytes 1769480 | tf_op jit(solution)/shard_map/ppermute | solution.py:56
where the time goes:
time: 74.5 us; the launch traced here: 74.3 us
  blocking collectives  35.3 us (47%)
  starting transfers between devices  20.7 us (28%)
  Pallas kernels  8.44 us (11%)
  waiting for transfers between devices  7.97 us (11%)
  local copies, waits for them, and re-layouts  1.15 us (2%)
  between operations  0.76 us (1%)
    all_to_all x2, blocking collectives, trade(): lax.all_to_all(blocks, BOTH, 0, 0, axis_index_groups=SLABS, tiled=True)  35.3 us
    ppermute x5, starting transfers between devices, send(): return lax.ppermute(value, BOTH, pairs)  15.4 us
    pallas_call x11, Pallas kernels, call(): pl.pallas_call(kernel, out_shape=outs, in_specs=specs, out_specs=jax.tree...  8.44 us
    ppermute x5, waiting for transfers between devices, send(): return lax.ppermute(value, BOTH, pairs)  3.64 us
    ppermute x1, starting transfers between devices, local(): even = lax.ppermute(even, 'lon', chain(0, True))  3.33 us
    ppermute x1, waiting for transfers between devices, local(): odd = lax.ppermute(odd, 'lon', chain(1, True))  2.26 us
    ppermute x1, waiting for transfers between devices, local(): even = lax.ppermute(even, 'lat', chain(0, False))  2.07 us
  transfers between devices with their start and end apart: 9, of which 5 were waited for; matrix products, arithmetic and copies ran while one was open for 0% of the time, Pallas kernels for 8%

commit v1 on v0

--- a/solution.py
+++ b/solution.py
@@ -72,7 +72,7 @@
     return max(0, 2 * u - 4) // 4, min(11, 2 * u + 5) // 4
 
 
-def rim_kernel(block_ref, even_ref, odd_ref, ext_ref):
+def rim_kernel(block_ref, odd_ref, even_ref, ext_ref):
     first = core_of() == 0
     west, east = block_ref[:, :8], block_ref[:, 37:]
     even_ref[...] = jnp.where(first, east, west)
@@ -81,7 +81,7 @@
     ext_ref[:, 8:53] = block_ref[...]
 
 
-def extend_kernel(block_ref, even_ref, odd_ref, ext_ref, to_even_ref, to_odd_ref):
+def extend_kernel(block_ref, odd_ref, even_ref, ext_ref, to_even_ref, to_odd_ref):
     first = core_of() == 0
     even, odd = even_ref[...], odd_ref[...]
     ext_ref[...] = block_ref[...]
@@ -269,12 +269,12 @@
 
 def local(features, cotangent, weights, quad_weights, reach_table):
     slab = shape((12, 8, 256), BF16)
-    even, odd, ext = call(
+    odd, even, ext = call(
         rim_kernel, (slab, slab, shape((12, 64, 256), BF16)), whole(1), cotangent,
         flops=2 * 10**10, bytes_accessed=10**6,
     )
+    odd = lax.ppermute(odd, "lon", chain(1, True))
     even = lax.ppermute(even, "lon", chain(0, True))
-    odd = lax.ppermute(odd, "lon", chain(1, True))
     band, rims, feat, feat_edge = call(
         band_kernel,
         (
@@ -286,10 +286,10 @@
             pltpu.VMEM((12, WIDE, 256), BF16), pltpu.VMEM((84 * WIN, 192), BF16), pltpu.VMEM((84, 32, 128), F32),
         ],
     )
-    even, odd, band = lax.optimization_barrier((even, odd, band))
+    odd, even, band = lax.optimization_barrier((odd, even, band))
     rim = shape((4, 64, 256), BF16)
     ext, even, odd = call(
-        extend_kernel, (shape((12, 64, 256), BF16), rim, rim), whole(3), ext, even, odd
+        extend_kernel, (shape((12, 64, 256), BF16), rim, rim), whole(3), ext, odd, even
     )
     even = lax.ppermute(even, "lat", chain(0, False))
     odd = lax.ppermute(odd, "lat", chain(1, False))

time: 74.5 us -> 74.3 us (level)
  waiting for transfers between devices: 7.97 us -> 4.47 us
  starting transfers between devices: 20.7 us -> 24.1 us
    ppermute x1, starting transfers between devices: 0.01 us -> 2.69 us  [local(): odd = lax.ppermute(odd, 'lon', chain(1, True))]
    ppermute x1, waiting for transfers between devices: 2.26 us -> 0.01 us  [local(): odd = lax.ppermute(odd, 'lon', chain(1, True))]
    ppermute x1, waiting for transfers between devices: 2.07 us -> 0.8 us  [local(): even = lax.ppermute(even, 'lat', chain(0, False))]
    ppermute x1, starting transfers between devices: 1.28 us -> 2.54 us  [local(): even = lax.ppermute(even, 'lat', chain(0, False))]
    ppermute x1, starting transfers between devices: 3.33 us -> 2.28 us  [local(): even = lax.ppermute(even, 'lon', chain(0, True))]
  transfers between devices with their start and end apart: 9 -> 9, of which waited for: 5 -> 4; matrix products, arithmetic and copies ran while one was open for 0% -> 0% of each run, Pallas kernels for 8% -> 8%
where the time goes in v1:
time: 74.3 us; the launch traced here: 74.1 us
  blocking collectives  35.1 us (47%)
  starting transfers between devices  24.1 us (32%)
  Pallas kernels  8.44 us (11%)
  waiting for transfers between devices  4.47 us (6%)
  local copies, waits for them, and re-layouts  1.15 us (2%)
  between operations  0.75 us (1%)
    all_to_all x2, blocking collectives, trade(): lax.all_to_all(blocks, BOTH, 0, 0, axis_index_groups=SLABS, tiled=True)  35.1 us
    ppermute x5, starting transfers between devices, send(): return lax.ppermute(value, BOTH, pairs)  15.9 us
    pallas_call x11, Pallas kernels, call(): pl.pallas_call(kernel, out_shape=outs, in_specs=specs, out_specs=jax.tree...  8.44 us
    ppermute x5, waiting for transfers between devices, send(): return lax.ppermute(value, BOTH, pairs)  3.66 us
    ppermute x1, starting transfers between devices, local(): odd = lax.ppermute(odd, 'lon', chain(1, True))  2.69 us
    ppermute x1, starting transfers between devices, local(): even = lax.ppermute(even, 'lat', chain(0, False))  2.54 us
    ppermute x1, starting transfers between devices, local(): even = lax.ppermute(even, 'lon', chain(0, True))  2.28 us
  transfers between devices with their start and end apart: 9, of which 4 were waited for; matrix products, arithmetic and copies ran while one was open for 0% of the time, Pallas kernels for 8%

profile of v1, /device:TPU:1, one launch (start us, length us, event | category | flops | bytes accessed | tf_op | source)
XLA Modules:
  0.0 74.1 jit_solution(9230744780046565176)
XLA Ops:
  0.6 0.0 copy-start.2
  0.6 0.0 copy-start
  0.7 0.0 copy-start.1
  0.7 0.0 copy-start.4
  0.7 1.1 %copy-done.4 = bf16[12,45,256]{2,1,0:T(8,128)(2,1)S(1)} copy-done((bf16[12,45,256]{2,1,0:T(8,128)(2,1)S(1)}, bf16[12,45,256]{2,1,0:T(8,128)(2,1)}, u32[]{:S(2)}) %copy-start.4) | copy-done | bytes 276504
  1.7 0.1 shard_map.68
  1.8 2.7 %collective-permute-start = (bf16[12,8,256]{2,1,0:T(8,128)(2,1)S(1)}, bf16[12,8,256]{2,1,0:T(8,128)(2,1)S(1)}, u32[]{:S(2)}, u32[]{:S(2)}) collective-permute-start(bf16[12,8,256]{2,1,0:T(8,128)(2,1)S(1)} %get-tuple-element.29), channel_id=1, source_target_pairs={{0,15},{1,2},{2,1},{3,4},{4,3},{5,6},{6,5},{7,8},{8,7},{9,10},{10,... | collective-permute-start | bytes 147464 | tf_op jit(solution)/shard_map/ppermute | solution.py:276
  4.5 2.3 %collective-permute-start.1 = (bf16[12,8,256]{2,1,0:T(8,128)(2,1)S(1)}, bf16[12,8,256]{2,1,0:T(8,128)(2,1)S(1)}, u32[]{:S(2)}, u32[]{:S(2)}) collective-permute-start(bf16[12,8,256]{2,1,0:T(8,128)(2,1)S(1)} %get-tuple-element.30), channel_id=1, source_target_pairs={{0,1},{1,0},{2,3},{3,2},{4,5},{5,4},{6,7},{7,6},{8,9},{9,8},{10,11... | collective-permute-start | bytes 147464 | tf_op jit(solution)/shard_map/ppermute | solution.py:277
  6.8 0.0 copy-done.2
  6.8 0.0 copy-done
  6.8 0.0 copy-done.1
  6.8 1.2 %shard_map.69 = (bf16[6,288,384]{2,1,0:T(8,128)(2,1)S(1)}, bf16[4,288,128]{2,1,0:T(8,128)(2,1)S(1)}, bf16[256,192]{1,0:T(8,128)(2,1)S(1)}, bf16[256,384]{1,0:T(8,128)(2,1)S(1)}) custom-call(bf16[9,9,17,192]{3,2,1,0:T(8,128)(2,1)S(1)} %bitcast.2, s32[9,192]{1,0:T(8,128)S(1)} %bitcast.3, bf16[12,45,256]{2,1,0:T(8,128)(2,1)S(1)} %copy-done.1), custom_call_target="tpu_custom_call" | custom-call | tf_op jit(solution)/shard_map/pallas_call | solution.py:254
  8.0 0.0 collective-permute-done.odd_ref
  8.0 0.0 collective-permute-done.1.even_ref
  8.0 0.1 shard_map.70
  8.1 2.5 %collective-permute-start.2 = (bf16[4,64,256]{2,1,0:T(8,128)(2,1)S(1)}, bf16[4,64,256]{2,1,0:T(8,128)(2,1)S(1)}, u32[]{:S(2)}, u32[]{:S(2)}) collective-permute-start(bf16[4,64,256]{2,1,0:T(8,128)(2,1)S(1)} %get-tuple-element.34), channel_id=1, source_target_pairs={{0,16},{16,0},{32,48},{48,32},{64,80},{80,64},{96,112},{112,96},{1... | collective-permute-start | bytes 393224 | tf_op jit(solution)/shard_map/ppermute | solution.py:294
  10.6 0.7 collective-permute-start.3
  11.3 1.4 %shard_map.71 = (bf16[9,192,256]{2,1,0:T(8,128)(2,1)S(1)}, f32[4,3,288,256]{3,2,1,0:T(8,128)S(1)}, f32[9,256,256]{2,1,0:T(8,128)S(1)}) custom-call(bf16[12,64,256]{2,1,0:T(8,128)(2,1)S(1)} %get-tuple-element.36.ext_ref, bf16[6,288,384]{2,1,0:T(8,128)(2,1)S(1)} %get-tuple-element.37.band_ref, bf16[256,192]{1,0:T(8,128)(2,1)S(1)} %get-tuple-element.38.feat_ref), custom_call_target="tpu_custom_call" | custom-call | flops 1000000 | bytes 1000000 | tf_op jit(solution)/shard_map/pallas_call | solution.py:254
  12.7 0.8 %collective-permute-done.2.even_ref = bf16[4,64,256]{2,1,0:T(8,128)(2,1)S(1)} collective-permute-done((bf16[4,64,256]{2,1,0:T(8,128)(2,1)S(1)}, bf16[4,64,256]{2,1,0:T(8,128)(2,1)S(1)}, u32[]{:S(2)}, u32[]{:S(2)}) %collective-permute-start.2) | collective-permute-done | bytes 131104 | tf_op jit(solution)/shard_map/ppermute | solution.py:294
  13.5 0.0 collective-permute-done.3.odd_ref
  13.5 1.1 %shard_map.72 = (bf16[9,384,256]{2,1,0:T(8,128)(2,1)S(1)}, bf16[9,128,256]{2,1,0:T(8,128)(2,1)S(1)}) custom-call(bf16[4,64,256]{2,1,0:T(8,128)(2,1)S(1)} %collective-permute-done.2.even_ref, bf16[4,64,256]{2,1,0:T(8,128)(2,1)S(1)} %collective-permute-done.3.odd_ref, bf16[4,288,128]{2,1,0:T(8,128)(2,1)S(1)} %get-tuple-element.42.rim_ref, ...), custom_call_target="tpu_custom_call" | custom-call | tf_op jit(solution)/shard_map/pallas_call | solution.py:254
  14.6 4.0 %collective-permute-start.4 = (bf16[9,128,256]{2,1,0:T(8,128)(2,1)S(1)}, bf16[9,128,256]{2,1,0:T(8,128)(2,1)S(1)}, u32[]{:S(2)}, u32[]{:S(2)}) collective-permute-start(bf16[9,128,256]{2,1,0:T(8,128)(2,1)S(1)} %get-tuple-element.47), channel_id=1, source_target_pairs={{0,1},{1,0},{2,3},{3,2},{4,5},{5,4},{6,7},{7,6},{8,9},{9,8},{10,11... | collective-permute-start | bytes 1769480 | tf_op jit(solution)/shard_map/ppermute | solution.py:56
  18.6 0.5 shard_map.73.keep_ref
  19.0 0.0 copy-start.3
  19.0 1.1 %collective-permute-done.4.got_ref = bf16[9,128,256]{2,1,0:T(8,128)(2,1)S(1)} collective-permute-done((bf16[9,128,256]{2,1,0:T(8,128)(2,1)S(1)}, bf16[9,128,256]{2,1,0:T(8,128)(2,1)S(1)}, u32[]{:S(2)}, u32[]{:S(2)}) %collective-permute-start.4) | collective-permute-done | bytes 589856 | tf_op jit(solution)/shard_map/ppermute | solution.py:56
  20.2 0.1 shard_map.74
  20.3 21.4 %all_to_all.10.got_ref = bf16[32,9,8,128]{3,2,1,0:T(8,128)(2,1)S(1)} all-to-all(bf16[32,9,8,128]{3,2,1,0:T(8,128)(2,1)S(1)} %shard_map.74), channel_id=1, replica_groups={{0,2,4,6,8,10,12,14,16,18,20,22,24,26,28,30,32,34,36,38,40,42,44,46,48,..., dimensions={0} | all-to-all | bytes 1179648 | tf_op jit(solution)/shard_map/all_to_all | solution.py:60
  41.7 0.1 shard_map.75
  41.8 4.8 %collective-permute-start.7 = (bf16[9,8,128]{2,1,0:T(8,128)(2,1)S(1)}, bf16[9,8,128]{2,1,0:T(8,128)(2,1)S(1)}, u32[]{:S(2)}, u32[]{:S(2)}) collective-permute-start(bf16[9,8,128]{2,1,0:T(8,128)(2,1)S(1)} %shard_map.75), channel_id=1, source_target_pairs={{0,192},{1,193},{2,194},{3,195},{4,196},{5,197},{6,198},{7,199},{8... | collective-permute-start | bytes 55304 | tf_op jit(solution)/shard_map/ppermute | solution.py:56
  46.5 2.8 %collective-permute-start.6 = (bf16[9,8,128]{2,1,0:T(8,128)(2,1)S(1)}, bf16[9,8,128]{2,1,0:T(8,128)(2,1)S(1)}, u32[]{:S(2)}, u32[]{:S(2)}) collective-permute-start(bf16[9,8,128]{2,1,0:T(8,128)(2,1)S(1)} %shard_map.75), channel_id=1, source_target_pairs={{0,128},{1,129},{2,130},{3,131},{4,132},{5,133},{6,134},{7,135},{8... | collective-permute-start | bytes 55304 | tf_op jit(solution)/shard_map/ppermute | solution.py:56
  49.4 0.0 collective-permute-start.5
  49.4 0.0 copy-done.3
  49.4 1.7 %shard_map.76 = bf16[12,45,256]{2,1,0:T(8,128)(2,1)} custom-call(bf16[9,192,256]{2,1,0:T(8,128)(2,1)S(1)} %get-tuple-element.50.middle_ref, bf16[9,384,256]{2,1,0:T(8,128)(2,1)S(1)} %get-tuple-element.51.y_ref.edge_ref, bf16[9,256,256]{2,1,0:T(8,128)(2,1)S(1)} %copy-done.3), custom_call_target="tpu_custom_call" | custom-call | flops 2000000000 | bytes 4000000 | tf_op jit(solution)/shard_map/pallas_call | solution.py:254
  51.1 0.0 collective-permute-done.7
  51.1 2.0 %collective-permute-done.6 = bf16[9,8,128]{2,1,0:T(8,128)(2,1)S(1)} collective-permute-done((bf16[9,8,128]{2,1,0:T(8,128)(2,1)S(1)}, bf16[9,8,128]{2,1,0:T(8,128)(2,1)S(1)}, u32[]{:S(2)}, u32[]{:S(2)}) %collective-permute-start.6) | collective-permute-done | bytes 18464 | tf_op jit(solution)/shard_map/ppermute | solution.py:56
  53.1 0.0 collective-permute-done.5
  53.1 0.1 broadcast_in_dim.3
  53.2 13.8 %all_to_all.11.blocks_ref = bf16[32,9,8,128]{3,2,1,0:T(8,128)(2,1)S(1)} all-to-all(bf16[32,9,8,128]{3,2,1,0:T(8,128)(2,1)S(1)} %broadcast_in_dim.3), channel_id=1, replica_groups={{0,2,4,6,8,10,12,14,16,18,20,22,24,26,28,30,32,34,36,38,40,42,44,46,48,..., dimensions={0} | all-to-all | bytes 1179648 | tf_op jit(solution)/shard_map/all_to_all | solution.py:60
  66.9 4.4 %collective-permute-start.8 = (bf16[32,9,8,128]{3,2,1,0:T(8,128)(2,1)S(1)}, bf16[32,9,8,128]{3,2,1,0:T(8,128)(2,1)S(1)}, u32[]{:S(2)}, u32[]{:S(2)}) collective-permute-start(bf16[32,9,8,128]{3,2,1,0:T(8,128)(2,1)S(1)} %all_to_all.11.blocks_ref), channel_id=1, source_target_pairs={{0,1},{1,0},{2,3},{3,2},{4,5},{5,4},{6,7},{7,6},{8,9},{9,8},{10,11... | collective-permute-start | bytes 1769480 | tf_op jit(solution)/shard_map/ppermute | solution.py:56
  71.3 1.1 %shard_map.77.refs_0_ = f32[9,256,256]{2,1,0:T(8,128)} custom-call(bf16[32,9,8,128]{3,2,1,0:T(8,128)(2,1)S(1)} %all_to_all.11.blocks_ref), custom_call_target="tpu_custom_call" | custom-call | flops 1000000 | bytes 2000000 | tf_op jit(solution)/shard_map/pallas_call | solution.py:254
  72.4 0.5 collective-permute-done.8.blocks_ref
  72.9 1.1 %shard_map.78 = f32[9,256,256]{2,1,0:T(8,128)} custom-call(bf16[32,9,8,128]{3,2,1,0:T(8,128)(2,1)S(1)} %collective-permute-done.8.blocks_ref, f32[9,256,256]{2,1,0:T(8,128)} %shard_map.77.refs_0_), custom_call_target="tpu_custom_call", output_to_operand_aliasing={{}: (1, {})} | custom-call | flops 1000000 | bytes 2000000 | tf_op jit(solution)/shard_map/pallas_call | solution.py:254
  (1 shorter events, 0.0 us)
Async XLA Ops:
  0.6 6.1 %copy-start.2 = (s32[192,9]{0,1:T(8,128)S(1)}, s32[192,9]{0,1:T(8,128)}, u32[]{:S(2)}) copy-start(s32[192,9]{0,1:T(8,128)} %param.9) | copy-start | bytes 20740
  0.6 6.1 %copy-start = (bf16[9,192,9,17]{1,3,2,0:T(8,128)(2,1)S(1)}, bf16[9,192,9,17]{1,3,2,0:T(8,128)(2,1)}, u32[]{:S(2)}) copy-start(bf16[9,192,9,17]{1,3,2,0:T(8,128)(2,1)} %param.8) | copy-start | bytes 1586308
  0.7 6.1 %copy-start.1 = (bf16[12,45,256]{2,1,0:T(8,128)(2,1)S(1)}, bf16[12,45,256]{2,1,0:T(8,128)(2,1)}, u32[]{:S(2)}) copy-start(bf16[12,45,256]{2,1,0:T(8,128)(2,1)} %feat_ref.1) | copy-start | bytes 829444
  0.7 1.1 %copy-start.4 = (bf16[12,45,256]{2,1,0:T(8,128)(2,1)S(1)}, bf16[12,45,256]{2,1,0:T(8,128)(2,1)}, u32[]{:S(2)}) copy-start(bf16[12,45,256]{2,1,0:T(8,128)(2,1)} %block_ref.1) | copy-start | bytes 829444
  1.8 6.2 %collective-permute-start = (bf16[12,8,256]{2,1,0:T(8,128)(2,1)S(1)}, bf16[12,8,256]{2,1,0:T(8,128)(2,1)S(1)}, u32[]{:S(2)}, u32[]{:S(2)}) collective-permute-start(bf16[12,8,256]{2,1,0:T(8,128)(2,1)S(1)} %get-tuple-element.29), channel_id=1, source_target_pairs={{0,15},{1,2},{2,1},{3,4},{4,3},{5,6},{6,5},{7,8},{8,7},{9,10},{10,... | collective-permute-start | bytes 147464 | tf_op jit(solution)/shard_map/ppermute | solution.py:276
  4.5 3.5 %collective-permute-start.1 = (bf16[12,8,256]{2,1,0:T(8,128)(2,1)S(1)}, bf16[12,8,256]{2,1,0:T(8,128)(2,1)S(1)}, u32[]{:S(2)}, u32[]{:S(2)}) collective-permute-start(bf16[12,8,256]{2,1,0:T(8,128)(2,1)S(1)} %get-tuple-element.30), channel_id=1, source_target_pairs={{0,1},{1,0},{2,3},{3,2},{4,5},{5,4},{6,7},{7,6},{8,9},{9,8},{10,11... | collective-permute-start | bytes 147464 | tf_op jit(solution)/shard_map/ppermute | solution.py:277
  8.1 5.4 %collective-permute-start.2 = (bf16[4,64,256]{2,1,0:T(8,128)(2,1)S(1)}, bf16[4,64,256]{2,1,0:T(8,128)(2,1)S(1)}, u32[]{:S(2)}, u32[]{:S(2)}) collective-permute-start(bf16[4,64,256]{2,1,0:T(8,128)(2,1)S(1)} %get-tuple-element.34), channel_id=1, source_target_pairs={{0,16},{16,0},{32,48},{48,32},{64,80},{80,64},{96,112},{112,96},{1... | collective-permute-start | bytes 393224 | tf_op jit(solution)/shard_map/ppermute | solution.py:294
  10.6 2.9 %collective-permute-start.3 = (bf16[4,64,256]{2,1,0:T(8,128)(2,1)S(1)}, bf16[4,64,256]{2,1,0:T(8,128)(2,1)S(1)}, u32[]{:S(2)}, u32[]{:S(2)}) collective-permute-start(bf16[4,64,256]{2,1,0:T(8,128)(2,1)S(1)} %get-tuple-element.35), channel_id=1, source_target_pairs={{16,32},{32,16},{48,64},{64,48},{80,96},{96,80},{112,128},{128,112... | collective-permute-start | bytes 393224 | tf_op jit(solution)/shard_map/ppermute | solution.py:295
  14.6 5.6 %collective-permute-start.4 = (bf16[9,128,256]{2,1,0:T(8,128)(2,1)S(1)}, bf16[9,128,256]{2,1,0:T(8,128)(2,1)S(1)}, u32[]{:S(2)}, u32[]{:S(2)}) collective-permute-start(bf16[9,128,256]{2,1,0:T(8,128)(2,1)S(1)} %get-tuple-element.47), channel_id=1, source_target_pairs={{0,1},{1,0},{2,3},{3,2},{4,5},{5,4},{6,7},{7,6},{8,9},{9,8},{10,11... | collective-permute-start | bytes 1769480 | tf_op jit(solution)/shard_map/ppermute | solution.py:56
  19.0 30.3 %copy-start.3 = (bf16[9,256,256]{2,1,0:T(8,128)(2,1)S(1)}, bf16[9,256,256]{2,1,0:T(8,128)(2,1)}, u32[]{:S(2)}) copy-start(bf16[9,256,256]{2,1,0:T(8,128)(2,1)} %w_ref.1) | copy-start | bytes 3538948
  41.8 9.3 %collective-permute-start.7 = (bf16[9,8,128]{2,1,0:T(8,128)(2,1)S(1)}, bf16[9,8,128]{2,1,0:T(8,128)(2,1)S(1)}, u32[]{:S(2)}, u32[]{:S(2)}) collective-permute-start(bf16[9,8,128]{2,1,0:T(8,128)(2,1)S(1)} %shard_map.75), channel_id=1, source_target_pairs={{0,192},{1,193},{2,194},{3,195},{4,196},{5,197},{6,198},{7,199},{8... | collective-permute-start | bytes 55304 | tf_op jit(solution)/shard_map/ppermute | solution.py:56
  46.5 6.5 %collective-permute-start.6 = (bf16[9,8,128]{2,1,0:T(8,128)(2,1)S(1)}, bf16[9,8,128]{2,1,0:T(8,128)(2,1)S(1)}, u32[]{:S(2)}, u32[]{:S(2)}) collective-permute-start(bf16[9,8,128]{2,1,0:T(8,128)(2,1)S(1)} %shard_map.75), channel_id=1, source_target_pairs={{0,128},{1,129},{2,130},{3,131},{4,132},{5,133},{6,134},{7,135},{8... | collective-permute-start | bytes 55304 | tf_op jit(solution)/shard_map/ppermute | solution.py:56
  49.4 3.7 %collective-permute-start.5 = (bf16[9,8,128]{2,1,0:T(8,128)(2,1)S(1)}, bf16[9,8,128]{2,1,0:T(8,128)(2,1)S(1)}, u32[]{:S(2)}, u32[]{:S(2)}) collective-permute-start(bf16[9,8,128]{2,1,0:T(8,128)(2,1)S(1)} %shard_map.75), channel_id=1, source_target_pairs={{0,64},{1,65},{2,66},{3,67},{4,68},{5,69},{6,70},{7,71},{8,72},{9,... | collective-permute-start | bytes 55304 | tf_op jit(solution)/shard_map/ppermute | solution.py:56
  66.9 6.0 %collective-permute-start.8 = (bf16[32,9,8,128]{3,2,1,0:T(8,128)(2,1)S(1)}, bf16[32,9,8,128]{3,2,1,0:T(8,128)(2,1)S(1)}, u32[]{:S(2)}, u32[]{:S(2)}) collective-permute-start(bf16[32,9,8,128]{3,2,1,0:T(8,128)(2,1)S(1)} %all_to_all.11.blocks_ref), channel_id=1, source_target_pairs={{0,1},{1,0},{2,3},{3,2},{4,5},{5,4},{6,7},{7,6},{8,9},{9,8},{10,11... | collective-permute-start | bytes 1769480 | tf_op jit(solution)/shard_map/ppermute | solution.py:56

commit v2 on v0

--- a/solution.py
+++ b/solution.py
@@ -238,14 +238,18 @@
 
 
 def join_kernel(scale, other, blocks_ref, *refs):
-    out_ref, half_ref, sem = refs[-3:]
+    out_ref, half_ref, sems = refs[-3:]
     start = pl.multiple_of((core_of() ^ other) * 128, 128)
-    for j in range(32):
-        rows, cols = slice(j // 2 * 8, j // 2 * 8 + 8), slice(j % 2 * 128, j % 2 * 128 + 128)
-        half_ref[:, rows, cols] = blocks_ref[j].astype(F32) * scale
-    copy = pltpu.make_async_copy(half_ref, out_ref.at[:, pl.ds(start, 128), :], sem)
-    copy.start()
-    copy.wait()
+    copies = []
+    for part in range(2):
+        for j in range(16 * part, 16 * part + 16):
+            rows, cols = slice(j // 2 * 8, j // 2 * 8 + 8), slice(j % 2 * 128, j % 2 * 128 + 128)
+            half_ref[:, rows, cols] = blocks_ref[j].astype(F32) * scale
+        target = out_ref.at[:, pl.ds(pl.multiple_of(start + 64 * part, 64), 64), :]
+        copies.append(pltpu.make_async_copy(half_ref.at[:, 64 * part : 64 * part + 64, :], target, sems.at[part]))
+        copies[part].start()
+    for copy in copies:
+        copy.wait()
 
 
 def call(kernel, outs, specs, *args, out_spec=None, scratch=(), aliases=None, **cost):
@@ -322,7 +326,7 @@
     own = trade(jnp.broadcast_to(total.astype(BF16), blocks))
     got = send(own, CORE)
     scale = 1.0 / math.sqrt(192 * 720)
-    scratch = [pltpu.VMEM(halves, F32), pltpu.SemaphoreType.DMA]
+    scratch = [pltpu.VMEM(halves, F32), pltpu.SemaphoreType.DMA((2,))]
     full = shape((9, 256, 256), F32)
     grad_weight = call(
         functools.partial(join_kernel, scale, 0), full, whole(1), own,

time: 74.5 us -> 74.5 us (level)
  no operation moved by 1% of the time
where the time goes in v2:
time: 74.5 us; the launch traced here: 74.3 us
  blocking collectives  35.3 us (47%)
  starting transfers between devices  20.7 us (28%)
  Pallas kernels  8.35 us (11%)
  waiting for transfers between devices  8.02 us (11%)
  local copies, waits for them, and re-layouts  1.15 us (2%)
  between operations  0.76 us (1%)
    all_to_all x2, blocking collectives, trade(): lax.all_to_all(blocks, BOTH, 0, 0, axis_index_groups=SLABS, tiled=True)  35.3 us
    ppermute x5, starting transfers between devices, send(): return lax.ppermute(value, BOTH, pairs)  15.4 us
    pallas_call x11, Pallas kernels, call(): pl.pallas_call(kernel, out_shape=outs, in_specs=specs, out_specs=jax.tree...  8.35 us
    ppermute x5, waiting for transfers between devices, send(): return lax.ppermute(value, BOTH, pairs)  3.69 us
    ppermute x1, starting transfers between devices, local(): even = lax.ppermute(even, 'lon', chain(0, True))  3.33 us
    ppermute x1, waiting for transfers between devices, local(): odd = lax.ppermute(odd, 'lon', chain(1, True))  2.26 us
    ppermute x1, waiting for transfers between devices, local(): even = lax.ppermute(even, 'lat', chain(0, False))  2.07 us
  transfers between devices with their start and end apart: 9, of which 5 were waited for; matrix products, arithmetic and copies ran while one was open for 0% of the time, Pallas kernels for 8%

profile of v2, /device:TPU:1, one launch (start us, length us, event | category | flops | bytes accessed | tf_op | source)
XLA Modules:
  0.0 74.3 jit_solution(10624841108223314098)
XLA Ops:
  0.6 0.0 copy-start.2
  0.6 0.0 copy-start
  0.7 0.0 copy-start.1
  0.7 0.0 copy-start.4
  0.7 1.1 %copy-done.4 = bf16[12,45,256]{2,1,0:T(8,128)(2,1)S(1)} copy-done((bf16[12,45,256]{2,1,0:T(8,128)(2,1)S(1)}, bf16[12,45,256]{2,1,0:T(8,128)(2,1)}, u32[]{:S(2)}) %copy-start.4) | copy-done | bytes 276504
  1.7 0.1 shard_map.68
  1.8 3.3 %collective-permute-start = (bf16[12,8,256]{2,1,0:T(8,128)(2,1)S(1)}, bf16[12,8,256]{2,1,0:T(8,128)(2,1)S(1)}, u32[]{:S(2)}, u32[]{:S(2)}) collective-permute-start(bf16[12,8,256]{2,1,0:T(8,128)(2,1)S(1)} %get-tuple-element.29), channel_id=1, source_target_pairs={{0,1},{1,0},{2,3},{3,2},{4,5},{5,4},{6,7},{7,6},{8,9},{9,8},{10,11... | collective-permute-start | bytes 147464 | tf_op jit(solution)/shard_map/ppermute | solution.py:280
  5.1 0.0 collective-permute-start.1
  5.1 0.0 copy-done.2
  5.1 0.0 copy-done
  5.1 0.0 copy-done.1
  5.1 1.2 %shard_map.69 = (bf16[6,288,384]{2,1,0:T(8,128)(2,1)S(1)}, bf16[4,288,128]{2,1,0:T(8,128)(2,1)S(1)}, bf16[256,192]{1,0:T(8,128)(2,1)S(1)}, bf16[256,384]{1,0:T(8,128)(2,1)S(1)}) custom-call(bf16[9,9,17,192]{3,2,1,0:T(8,128)(2,1)S(1)} %bitcast.2, s32[9,192]{1,0:T(8,128)S(1)} %bitcast.3, bf16[12,45,256]{2,1,0:T(8,128)(2,1)S(1)} %copy-done.1), custom_call_target="tpu_custom_call" | custom-call | tf_op jit(solution)/shard_map/pallas_call | solution.py:258
  6.4 0.0 collective-permute-done.even_ref
  6.4 2.3 %collective-permute-done.1.odd_ref = bf16[12,8,256]{2,1,0:T(8,128)(2,1)S(1)} collective-permute-done((bf16[12,8,256]{2,1,0:T(8,128)(2,1)S(1)}, bf16[12,8,256]{2,1,0:T(8,128)(2,1)S(1)}, u32[]{:S(2)}, u32[]{:S(2)}) %collective-permute-start.1) | collective-permute-done | bytes 49184 | tf_op jit(solution)/shard_map/ppermute | solution.py:281
  8.6 0.1 shard_map.70
  8.7 1.3 %collective-permute-start.2 = (bf16[4,64,256]{2,1,0:T(8,128)(2,1)S(1)}, bf16[4,64,256]{2,1,0:T(8,128)(2,1)S(1)}, u32[]{:S(2)}, u32[]{:S(2)}) collective-permute-start(bf16[4,64,256]{2,1,0:T(8,128)(2,1)S(1)} %get-tuple-element.34), channel_id=1, source_target_pairs={{0,16},{16,0},{32,48},{48,32},{64,80},{80,64},{96,112},{112,96},{1... | collective-permute-start | bytes 393224 | tf_op jit(solution)/shard_map/ppermute | solution.py:298
  10.0 0.7 collective-permute-start.3
  10.7 1.4 %shard_map.71 = (bf16[9,192,256]{2,1,0:T(8,128)(2,1)S(1)}, f32[4,3,288,256]{3,2,1,0:T(8,128)S(1)}, f32[9,256,256]{2,1,0:T(8,128)S(1)}) custom-call(bf16[12,64,256]{2,1,0:T(8,128)(2,1)S(1)} %get-tuple-element.36.ext_ref, bf16[6,288,384]{2,1,0:T(8,128)(2,1)S(1)} %get-tuple-element.37.band_ref, bf16[256,192]{1,0:T(8,128)(2,1)S(1)} %get-tuple-element.38.feat_ref), custom_call_target="tpu_custom_call" | custom-call | flops 1000000 | bytes 1000000 | tf_op jit(solution)/shard_map/pallas_call | solution.py:258
  12.1 2.1 %collective-permute-done.2.even_ref = bf16[4,64,256]{2,1,0:T(8,128)(2,1)S(1)} collective-permute-done((bf16[4,64,256]{2,1,0:T(8,128)(2,1)S(1)}, bf16[4,64,256]{2,1,0:T(8,128)(2,1)S(1)}, u32[]{:S(2)}, u32[]{:S(2)}) %collective-permute-start.2) | collective-permute-done | bytes 131104 | tf_op jit(solution)/shard_map/ppermute | solution.py:298
  14.1 0.0 collective-permute-done.3.odd_ref
  14.1 1.1 %shard_map.72 = (bf16[9,384,256]{2,1,0:T(8,128)(2,1)S(1)}, bf16[9,128,256]{2,1,0:T(8,128)(2,1)S(1)}) custom-call(bf16[4,64,256]{2,1,0:T(8,128)(2,1)S(1)} %collective-permute-done.2.even_ref, bf16[4,64,256]{2,1,0:T(8,128)(2,1)S(1)} %collective-permute-done.3.odd_ref, bf16[4,288,128]{2,1,0:T(8,128)(2,1)S(1)} %get-tuple-element.42.rim_ref, ...), custom_call_target="tpu_custom_call" | custom-call | tf_op jit(solution)/shard_map/pallas_call | solution.py:258
  15.2 3.4 %collective-permute-start.4 = (bf16[9,128,256]{2,1,0:T(8,128)(2,1)S(1)}, bf16[9,128,256]{2,1,0:T(8,128)(2,1)S(1)}, u32[]{:S(2)}, u32[]{:S(2)}) collective-permute-start(bf16[9,128,256]{2,1,0:T(8,128)(2,1)S(1)} %get-tuple-element.47), channel_id=1, source_target_pairs={{0,1},{1,0},{2,3},{3,2},{4,5},{5,4},{6,7},{7,6},{8,9},{9,8},{10,11... | collective-permute-start | bytes 1769480 | tf_op jit(solution)/shard_map/ppermute | solution.py:56
  18.6 0.5 shard_map.73.keep_ref
  19.1 0.0 copy-start.3
  19.1 1.1 %collective-permute-done.4.got_ref = bf16[9,128,256]{2,1,0:T(8,128)(2,1)S(1)} collective-permute-done((bf16[9,128,256]{2,1,0:T(8,128)(2,1)S(1)}, bf16[9,128,256]{2,1,0:T(8,128)(2,1)S(1)}, u32[]{:S(2)}, u32[]{:S(2)}) %collective-permute-start.4) | collective-permute-done | bytes 589856 | tf_op jit(solution)/shard_map/ppermute | solution.py:56
  20.3 0.1 shard_map.74
  20.4 21.6 %all_to_all.10.got_ref = bf16[32,9,8,128]{3,2,1,0:T(8,128)(2,1)S(1)} all-to-all(bf16[32,9,8,128]{3,2,1,0:T(8,128)(2,1)S(1)} %shard_map.74), channel_id=1, replica_groups={{0,2,4,6,8,10,12,14,16,18,20,22,24,26,28,30,32,34,36,38,40,42,44,46,48,..., dimensions={0} | all-to-all | bytes 1179648 | tf_op jit(solution)/shard_map/all_to_all | solution.py:60
  42.0 0.1 shard_map.75
  42.1 4.8 %collective-permute-start.7 = (bf16[9,8,128]{2,1,0:T(8,128)(2,1)S(1)}, bf16[9,8,128]{2,1,0:T(8,128)(2,1)S(1)}, u32[]{:S(2)}, u32[]{:S(2)}) collective-permute-start(bf16[9,8,128]{2,1,0:T(8,128)(2,1)S(1)} %shard_map.75), channel_id=1, source_target_pairs={{0,192},{1,193},{2,194},{3,195},{4,196},{5,197},{6,198},{7,199},{8... | collective-permute-start | bytes 55304 | tf_op jit(solution)/shard_map/ppermute | solution.py:56
  46.8 2.8 %collective-permute-start.6 = (bf16[9,8,128]{2,1,0:T(8,128)(2,1)S(1)}, bf16[9,8,128]{2,1,0:T(8,128)(2,1)S(1)}, u32[]{:S(2)}, u32[]{:S(2)}) collective-permute-start(bf16[9,8,128]{2,1,0:T(8,128)(2,1)S(1)} %shard_map.75), channel_id=1, source_target_pairs={{0,128},{1,129},{2,130},{3,131},{4,132},{5,133},{6,134},{7,135},{8... | collective-permute-start | bytes 55304 | tf_op jit(solution)/shard_map/ppermute | solution.py:56
  49.6 0.0 collective-permute-start.5
  49.6 0.0 copy-done.3
  49.6 1.7 %shard_map.76 = bf16[12,45,256]{2,1,0:T(8,128)(2,1)} custom-call(bf16[9,192,256]{2,1,0:T(8,128)(2,1)S(1)} %get-tuple-element.50.middle_ref, bf16[9,384,256]{2,1,0:T(8,128)(2,1)S(1)} %get-tuple-element.51.y_ref.edge_ref, bf16[9,256,256]{2,1,0:T(8,128)(2,1)S(1)} %copy-done.3), custom_call_target="tpu_custom_call" | custom-call | flops 2000000000 | bytes 4000000 | tf_op jit(solution)/shard_map/pallas_call | solution.py:258
  51.3 0.0 collective-permute-done.7
  51.3 2.0 %collective-permute-done.6 = bf16[9,8,128]{2,1,0:T(8,128)(2,1)S(1)} collective-permute-done((bf16[9,8,128]{2,1,0:T(8,128)(2,1)S(1)}, bf16[9,8,128]{2,1,0:T(8,128)(2,1)S(1)}, u32[]{:S(2)}, u32[]{:S(2)}) %collective-permute-start.6) | collective-permute-done | bytes 18464 | tf_op jit(solution)/shard_map/ppermute | solution.py:56
  53.3 0.0 collective-permute-done.5
  53.4 0.1 broadcast_in_dim.3
  53.4 13.8 %all_to_all.11.blocks_ref = bf16[32,9,8,128]{3,2,1,0:T(8,128)(2,1)S(1)} all-to-all(bf16[32,9,8,128]{3,2,1,0:T(8,128)(2,1)S(1)} %broadcast_in_dim.3), channel_id=1, replica_groups={{0,2,4,6,8,10,12,14,16,18,20,22,24,26,28,30,32,34,36,38,40,42,44,46,48,..., dimensions={0} | all-to-all | bytes 1179648 | tf_op jit(solution)/shard_map/all_to_all | solution.py:60
  67.2 4.4 %collective-permute-start.8 = (bf16[32,9,8,128]{3,2,1,0:T(8,128)(2,1)S(1)}, bf16[32,9,8,128]{3,2,1,0:T(8,128)(2,1)S(1)}, u32[]{:S(2)}, u32[]{:S(2)}) collective-permute-start(bf16[32,9,8,128]{3,2,1,0:T(8,128)(2,1)S(1)} %all_to_all.11.blocks_ref), channel_id=1, source_target_pairs={{0,1},{1,0},{2,3},{3,2},{4,5},{5,4},{6,7},{7,6},{8,9},{9,8},{10,11... | collective-permute-start | bytes 1769480 | tf_op jit(solution)/shard_map/ppermute | solution.py:56
  71.6 1.1 %shard_map.77.refs_0_ = f32[9,256,256]{2,1,0:T(8,128)} custom-call(bf16[32,9,8,128]{3,2,1,0:T(8,128)(2,1)S(1)} %all_to_all.11.blocks_ref), custom_call_target="tpu_custom_call" | custom-call | flops 1000000 | bytes 2000000 | tf_op jit(solution)/shard_map/pallas_call | solution.py:258
  72.7 0.5 collective-permute-done.8.blocks_ref
  73.2 1.1 %shard_map.78 = f32[9,256,256]{2,1,0:T(8,128)} custom-call(bf16[32,9,8,128]{3,2,1,0:T(8,128)(2,1)S(1)} %collective-permute-done.8.blocks_ref, f32[9,256,256]{2,1,0:T(8,128)} %shard_map.77.refs_0_), custom_call_target="tpu_custom_call", output_to_operand_aliasing={{}: (1, {})} | custom-call | flops 1000000 | bytes 2000000 | tf_op jit(solution)/shard_map/pallas_call | solution.py:258
  (1 shorter events, 0.0 us)
Async XLA Ops:
  0.6 4.5 %copy-start.2 = (s32[192,9]{0,1:T(8,128)S(1)}, s32[192,9]{0,1:T(8,128)}, u32[]{:S(2)}) copy-start(s32[192,9]{0,1:T(8,128)} %param.9) | copy-start | bytes 20740
  0.6 4.5 %copy-start = (bf16[9,192,9,17]{1,3,2,0:T(8,128)(2,1)S(1)}, bf16[9,192,9,17]{1,3,2,0:T(8,128)(2,1)}, u32[]{:S(2)}) copy-start(bf16[9,192,9,17]{1,3,2,0:T(8,128)(2,1)} %param.8) | copy-start | bytes 1586308
  0.7 4.5 %copy-start.1 = (bf16[12,45,256]{2,1,0:T(8,128)(2,1)S(1)}, bf16[12,45,256]{2,1,0:T(8,128)(2,1)}, u32[]{:S(2)}) copy-start(bf16[12,45,256]{2,1,0:T(8,128)(2,1)} %feat_ref.1) | copy-start | bytes 829444
  0.7 1.1 %copy-start.4 = (bf16[12,45,256]{2,1,0:T(8,128)(2,1)S(1)}, bf16[12,45,256]{2,1,0:T(8,128)(2,1)}, u32[]{:S(2)}) copy-start(bf16[12,45,256]{2,1,0:T(8,128)(2,1)} %block_ref.1) | copy-start | bytes 829444
  1.8 4.6 %collective-permute-start = (bf16[12,8,256]{2,1,0:T(8,128)(2,1)S(1)}, bf16[12,8,256]{2,1,0:T(8,128)(2,1)S(1)}, u32[]{:S(2)}, u32[]{:S(2)}) collective-permute-start(bf16[12,8,256]{2,1,0:T(8,128)(2,1)S(1)} %get-tuple-element.29), channel_id=1, source_target_pairs={{0,1},{1,0},{2,3},{3,2},{4,5},{5,4},{6,7},{7,6},{8,9},{9,8},{10,11... | collective-permute-start | bytes 147464 | tf_op jit(solution)/shard_map/ppermute | solution.py:280
  5.1 3.5 %collective-permute-start.1 = (bf16[12,8,256]{2,1,0:T(8,128)(2,1)S(1)}, bf16[12,8,256]{2,1,0:T(8,128)(2,1)S(1)}, u32[]{:S(2)}, u32[]{:S(2)}) collective-permute-start(bf16[12,8,256]{2,1,0:T(8,128)(2,1)S(1)} %get-tuple-element.30), channel_id=1, source_target_pairs={{0,15},{1,2},{2,1},{3,4},{4,3},{5,6},{6,5},{7,8},{8,7},{9,10},{10,... | collective-permute-start | bytes 147464 | tf_op jit(solution)/shard_map/ppermute | solution.py:281
  8.7 5.4 %collective-permute-start.2 = (bf16[4,64,256]{2,1,0:T(8,128)(2,1)S(1)}, bf16[4,64,256]{2,1,0:T(8,128)(2,1)S(1)}, u32[]{:S(2)}, u32[]{:S(2)}) collective-permute-start(bf16[4,64,256]{2,1,0:T(8,128)(2,1)S(1)} %get-tuple-element.34), channel_id=1, source_target_pairs={{0,16},{16,0},{32,48},{48,32},{64,80},{80,64},{96,112},{112,96},{1... | collective-permute-start | bytes 393224 | tf_op jit(solution)/shard_map/ppermute | solution.py:298
  10.0 4.1 %collective-permute-start.3 = (bf16[4,64,256]{2,1,0:T(8,128)(2,1)S(1)}, bf16[4,64,256]{2,1,0:T(8,128)(2,1)S(1)}, u32[]{:S(2)}, u32[]{:S(2)}) collective-permute-start(bf16[4,64,256]{2,1,0:T(8,128)(2,1)S(1)} %get-tuple-element.35), channel_id=1, source_target_pairs={{16,32},{32,16},{48,64},{64,48},{80,96},{96,80},{112,128},{128,112... | collective-permute-start | bytes 393224 | tf_op jit(solution)/shard_map/ppermute | solution.py:299
  15.2 5.1 %collective-permute-start.4 = (bf16[9,128,256]{2,1,0:T(8,128)(2,1)S(1)}, bf16[9,128,256]{2,1,0:T(8,128)(2,1)S(1)}, u32[]{:S(2)}, u32[]{:S(2)}) collective-permute-start(bf16[9,128,256]{2,1,0:T(8,128)(2,1)S(1)} %get-tuple-element.47), channel_id=1, source_target_pairs={{0,1},{1,0},{2,3},{3,2},{4,5},{5,4},{6,7},{7,6},{8,9},{9,8},{10,11... | collective-permute-start | bytes 1769480 | tf_op jit(solution)/shard_map/ppermute | solution.py:56
  19.1 30.5 %copy-start.3 = (bf16[9,256,256]{2,1,0:T(8,128)(2,1)S(1)}, bf16[9,256,256]{2,1,0:T(8,128)(2,1)}, u32[]{:S(2)}) copy-start(bf16[9,256,256]{2,1,0:T(8,128)(2,1)} %w_ref.1) | copy-start | bytes 3538948
  42.1 9.3 %collective-permute-start.7 = (bf16[9,8,128]{2,1,0:T(8,128)(2,1)S(1)}, bf16[9,8,128]{2,1,0:T(8,128)(2,1)S(1)}, u32[]{:S(2)}, u32[]{:S(2)}) collective-permute-start(bf16[9,8,128]{2,1,0:T(8,128)(2,1)S(1)} %shard_map.75), channel_id=1, source_target_pairs={{0,192},{1,193},{2,194},{3,195},{4,196},{5,197},{6,198},{7,199},{8... | collective-permute-start | bytes 55304 | tf_op jit(solution)/shard_map/ppermute | solution.py:56
  46.8 6.5 %collective-permute-start.6 = (bf16[9,8,128]{2,1,0:T(8,128)(2,1)S(1)}, bf16[9,8,128]{2,1,0:T(8,128)(2,1)S(1)}, u32[]{:S(2)}, u32[]{:S(2)}) collective-permute-start(bf16[9,8,128]{2,1,0:T(8,128)(2,1)S(1)} %shard_map.75), channel_id=1, source_target_pairs={{0,128},{1,129},{2,130},{3,131},{4,132},{5,133},{6,134},{7,135},{8... | collective-permute-start | bytes 55304 | tf_op jit(solution)/shard_map/ppermute | solution.py:56
  49.6 3.7 %collective-permute-start.5 = (bf16[9,8,128]{2,1,0:T(8,128)(2,1)S(1)}, bf16[9,8,128]{2,1,0:T(8,128)(2,1)S(1)}, u32[]{:S(2)}, u32[]{:S(2)}) collective-permute-start(bf16[9,8,128]{2,1,0:T(8,128)(2,1)S(1)} %shard_map.75), channel_id=1, source_target_pairs={{0,64},{1,65},{2,66},{3,67},{4,68},{5,69},{6,70},{7,71},{8,72},{9,... | collective-permute-start | bytes 55304 | tf_op jit(solution)/shard_map/ppermute | solution.py:56
  67.2 6.0 %collective-permute-start.8 = (bf16[32,9,8,128]{3,2,1,0:T(8,128)(2,1)S(1)}, bf16[32,9,8,128]{3,2,1,0:T(8,128)(2,1)S(1)}, u32[]{:S(2)}, u32[]{:S(2)}) collective-permute-start(bf16[32,9,8,128]{3,2,1,0:T(8,128)(2,1)S(1)} %all_to_all.11.blocks_ref), channel_id=1, source_target_pairs={{0,1},{1,0},{2,3},{3,2},{4,5},{5,4},{6,7},{7,6},{8,9},{9,8},{10,11... | collective-permute-start | bytes 1769480 | tf_op jit(solution)/shard_map/ppermute | solution.py:56
